TPU v7x, 32 devices: a whole 2x2x4 slice. The times are simulated.
32 devices in a mesh: nodes: 32 (over z, y, x, core).
Axes of the slice: x: 2, y: 2, z: 4, core: 2. Of those that a mesh axis runs over, the one named last changes fastest.
Arguments:
- node_table: float32 [307200, 400], P('nodes'), may hold values from -6 to 6
- batch_nodes: int32 [65536], P('nodes'), may hold values from 0 to 307199, as said below
- send_counts: int32 [32, 32], P('nodes'), may hold values from 1 to 64, as said below
- labels: int32 [65536], P('nodes'), may hold values from 0 to 46
- hop_weight: float32 [4, 100, 512], replicated, may hold values from -0.625 to 0.625
- hop_gain: float32 [4, 512], replicated, may hold values from 0.5 to 1.5
- hop_shift: float32 [4, 512], replicated, may hold values from -3 to 3
- hop_slope: float32 [4, 512], replicated, may hold values from 0 to 0.5
- cat_slope: float32 [2048], replicated, may hold values from 0 to 0.5
- mid_weight: float32 [2048, 512], replicated, may hold values from -0.125 to 0.125
- mid_gain: float32 [512], replicated, may hold values from 0.5 to 1.5
- mid_shift: float32 [512], replicated, may hold values from -3 to 3
- mid_slope: float32 [512], replicated, may hold values from 0 to 0.5
- out_weight: float32 [512, 47], replicated, may hold values from -0.5 to 0.5
- out_bias: float32 [47], replicated, may hold values from -3 to 3
Outputs:
- mean_loss: float32 [], replicated
- hop_weight_grad: float32 [4, 100, 512], replicated
- hop_gain_grad: float32 [4, 512], replicated
- hop_shift_grad: float32 [4, 512], replicated
- hop_slope_grad: float32 [4, 512], replicated
- cat_slope_grad: float32 [2048], replicated
- mid_weight_grad: float32 [2048, 512], replicated
- mid_gain_grad: float32 [512], replicated
- mid_shift_grad: float32 [512], replicated
- mid_slope_grad: float32 [512], replicated
- out_weight_grad: float32 [512, 47], replicated
- out_bias_grad: float32 [47], replicated
Inputs may be any that keep to these rules, and one draw needn't show every extreme that they name: `batch_nodes`: the slot at position (s * 32 + d) * 64 + k names a node of owner d, between d * 9600 and (d + 1) * 9600 - 1; only slots with k < send_counts[s, d] belong to the batch. `send_counts`: in every draw one owner, drawn from the seed, has 64 live slots from every device.
All inputs are finite; a program needn't handle non-finite values.
Results may differ from a plain program's by a relative error of at most 0.0003.
Values sent between devices are 32-bit elements; how exact they have to be, the bound alone decides.
A program may use at most 192 MiB of HBM per device.

v0:
```python
import functools

import jax
import jax.numpy as jnp
from jax import lax
from jax.experimental import pallas as pl
from jax.experimental.pallas import tpu as pltpu
from jax.sharding import PartitionSpec as P

MESH = pl.DeviceIdType.MESH
F32, BF16 = jnp.float32, jnp.bfloat16
NN = (((1,), (0,)), ((), ()))
NT = (((1,), (1,)), ((), ()))
W = 512
WIN = 256


def win_start(hop):
    return max(hop - 1, 0) * 128


def split(values):
    high = values.astype(BF16)
    return high, (values - high.astype(F32)).astype(BF16)


def dot(a, b, dims):
    return lax.dot_general(a, b, dims, preferred_element_type=F32)


def dot3(ah, al, bh, bl, dims=NN):
    (da,), (db,) = dims[0]
    return dot(
        jnp.concatenate([ah, al, ah], da), jnp.concatenate([bh, bh, bl], db), dims
    )


def wide(column):
    return jnp.concatenate([column] * (W // 128), axis=1)


def fold(values):
    out = values[:, 0:128]
    for tile in range(1, W // 128):
        out = out + values[:, tile * 128 : (tile + 1) * 128]
    return out


def lane_sum(values):
    return jnp.broadcast_to(jnp.sum(values, axis=1, keepdims=True), values.shape)


def to_row(column):
    return column.T[0:1, :]


def to_column(row):
    return jnp.broadcast_to(row, (128, row.shape[1])).T


def main_kernel(
    n,
    slots,
    table,
    nodes,
    labels,
    counts,
    weights,
    mid_weight,
    gain,
    shift,
    slope,
    cat_slope,
    mid_gain,
    mid_shift,
    mid_slope,
    out_t,
    bias,
    mid_sum,
    rest_sum,
    stats,
    cat_hbm,
    tab,
    x,
    dwm,
    xh,
    xl,
    wmh,
    wml,
    pgh,
    pgl,
    cath,
    catl,
    par,
    mcol,
    acc,
    vec,
    mask,
    lab,
    delta,
    ext,
    res,
    own,
    hop_grad,
    cg,
    ids,
    pack,
    got0,
    got1,
    got2,
    got3,
    send_sem,
    recv_sem,
    sum_send,
    sum_recv,
    part_send,
    part_recv,
    credit,
    freed,
    table_sem,
    load_sem,
    cat_sem,
):
    me = lax.axis_index("nodes")
    rows = slots * n
    blocks = rows // W
    feats, node_rows = table.shape
    hops = 4
    chunk = next(c for c in (512, 384, 256, 128) if node_rows % c == 0)
    chunks = node_rows // chunk
    depth = min(dwm.shape[0] // feats, chunks)

    def peer(k):
        return lax.rem(me + k, n)

    def table_copy(i, slot):
        return pltpu.make_async_copy(
            table.at[:, pl.ds(pl.multiple_of(i * chunk, 128), chunk)],
            dwm.at[pl.ds(pl.multiple_of(slot * feats, 8), feats), 0:chunk],
            table_sem.at[slot],
        )

    def send_all(buf, e):
        @pl.loop(1, n)
        def _(k):
            pltpu.make_async_remote_copy(
                buf.at[me], buf.at[me], send_sem.at[e], recv_sem.at[e],
                device_id=(peer(k),), device_id_type=MESH,
            ).start()

    def wait_all(buf, e):
        others = buf.at[pl.ds(0, n - 1)]
        pltpu.make_async_copy(others, others, send_sem.at[e]).wait()
        pltpu.make_async_copy(others, others, recv_sem.at[e]).wait()

    for i in range(depth):
        table_copy(i, i).start()
    weight_load = pltpu.make_async_copy(mid_weight, x, load_sem.at[0])
    weight_load.start()

    barrier = pltpu.get_barrier_semaphore()

    @pl.loop(1, n)
    def _(k):
        pl.semaphore_signal(barrier, inc=1, device_id=(peer(k),), device_id_type=MESH)

    ext[...] = jnp.zeros_like(ext)
    for h in range(hops):
        here = slice(h * W, (h + 1) * W)
        par[0, here, :] = to_column(gain[h : h + 1, :])
        par[1, here, :] = to_column(shift[h : h + 1, :])
        par[2, here, :] = to_column(0.5 + 0.5 * slope[h : h + 1, :])
        par[3, here, :] = to_column(0.5 + 0.5 * cat_slope[0:1, here])
    for j, row in enumerate((mid_gain, mid_shift, mid_slope)):
        mcol[j] = to_column(row[...])

    per = 128 // slots
    lane8 = lax.broadcasted_iota(jnp.int32, (8, 128), 1)

    @pl.loop(0, rows // 128)
    def _(j):
        own = jnp.broadcast_to(nodes[pl.ds(j, 1), :], (8, 128))
        names = jnp.broadcast_to(labels[pl.ds(j, 1), :], (8, 128))
        for q in range(per):
            d = j * per + q
            turn = (128 - q * slots) % 128
            ids_row = pltpu.roll(own, turn, 1) if q else own
            names_row = pltpu.roll(names, turn, 1) if q else names
            names_row = jnp.where(lane8 == 127, counts[0, d], names_row)
            place_row = jnp.clip(ids_row - d * node_rows, 0, node_rows - 1)
            pack[d, 0:1, :] = place_row[0:1, :]
            pack[d, 1:2, :] = names_row[0:1, :]

    pl.semaphore_wait(barrier, n - 1)
    got0[me] = pack[me]

    @pl.loop(1, n)
    def _(k):
        pltpu.make_async_remote_copy(
            pack.at[peer(k)], got0.at[me], send_sem.at[0], recv_sem.at[0],
            device_id=(peer(k),), device_id_type=MESH,
        ).start()

    @pl.loop(0, chunks)
    def _(i):
        slot = lax.rem(i, depth)
        table_copy(i, slot).wait()
        for k in range(chunk // 128):
            tab[pl.ds(pl.multiple_of(i * chunk + k * 128, 128), 128), 0:feats] = dwm[
                pl.ds(pl.multiple_of(slot * feats, 8), feats), k * 128 : (k + 1) * 128
            ].T

        @pl.when(i + depth < chunks)
        def _():
            table_copy(i + depth, slot).start()

    plain_load = pltpu.make_async_copy(mid_weight, dwm, load_sem.at[0])
    width = weights.shape[0]
    for h in range(hops):
        start = h * width - win_start(h)
        ext[0:WIN, :] = jnp.zeros((WIN, W), F32)
        ext[start : start + width, :] = weights[:, h, :]
        high, low = split(ext[0:WIN, :].T)
        pgh[h * W : (h + 1) * W, 0:WIN] = high
        pgh[h * W : (h + 1) * W, WIN : 2 * WIN] = low

    weight_load.wait()
    for h in range(hops):
        high, low = split(x[h * W : (h + 1) * W, :].T)
        wmh[h * W : (h + 1) * W, :] = high
        wml[h * W : (h + 1) * W, :] = low
    plain_load.start()

    wait_all(got0, 0)

    to_smem = pltpu.make_async_copy(got0, ids, load_sem.at[1])
    to_smem.start()
    to_smem.wait()

    step = min(slots, 16)

    @pl.loop(0, n)
    def _(s):
        @pl.loop(0, slots // step)
        def _(g):
            for k in range(step):
                at = g * step + k
                x[pl.ds(s * slots + at, 1), :] = tab[pl.ds(ids[s, 0, at], 1), :]

    @pl.loop(0, rows // 128)
    def _(j):
        live = jnp.zeros((8, 128), F32)
        names = jnp.zeros((8, 128), jnp.int32)
        for q in range(per):
            s = j * per + q
            mine = (lane8 >= q * slots) & (lane8 < (q + 1) * slots)
            live = live + jnp.where(
                mine & (lane8 < q * slots + ids[s, 1, 127]), 1.0, 0.0
            )
            row = jnp.broadcast_to(got0[s, 1:2, :], (8, 128))
            if q:
                row = pltpu.roll(row, q * slots, 1)
            names = jnp.where(mine, row, names)
        at = pl.ds(pl.multiple_of(j * 128, 128), 128)
        mask[0:1, at] = live[0:1, :]
        lab[0:1, at] = names[0:1, :]

    here_count = jnp.broadcast_to(
        jnp.sum(mask[...], axis=1, keepdims=True), (1, 128)
    )
    acc[0] = jnp.zeros((W, 128), F32)
    top_row = lax.broadcasted_iota(jnp.int32, (128, W), 0)

    @pl.loop(0, blocks)
    def _(b):
        at = pl.ds(pl.multiple_of(b * W, W), W)
        live = mask[0:1, at]
        for f in range(4):
            block = x[at, f * 128 : (f + 1) * 128].T
            if (f + 1) * 128 > feats:
                block = jnp.where(top_row < feats - f * 128, block, 0.0)
            tab[pl.ds(pl.multiple_of(b * W + f * 128, 128), 128), :] = block
            acc[0, f * 128 : (f + 1) * 128, :] += fold(block * live)

    mean_here = lane_sum(acc[0]) / here_count

    @pl.loop(0, blocks)
    def _(b):
        at = pl.ds(pl.multiple_of(b * W, W), W)
        live = mask[0:1, at]
        high, low = split((tab[at, :] - wide(mean_here)) * live)
        xh[:, at] = high
        xl[:, at] = low

    def pre_at(h, b):
        return pl.ds(pl.multiple_of((h * blocks + b) * W, W), W)

    for h in range(hops):
        wh = pgh[h * W : (h + 1) * W, 0:WIN]
        wl = pgh[h * W : (h + 1) * W, WIN : 2 * WIN]
        window = slice(win_start(h), win_start(h) + WIN)
        acc[h] = jnp.zeros((W, 128), F32)

        @pl.loop(0, blocks)
        def _(b):
            at = pl.ds(pl.multiple_of(b * W, W), W)
            pre = dot3(wh, wl, xh[window, at], xl[window, at])
            tab[pre_at(h, b), :] = pre
            acc[h] += fold(pre * pre)

    for h in range(hops):
        row = to_row(lane_sum(acc[h]))
        if h < 3:
            got1[me, 0:1, h * W : (h + 1) * W] = row
        else:
            got1[me, 1:2, 0:W] = row
    got1[me, 1:2, W : 2 * W] = to_row(mean_here)
    got1[me, 1:2, 2 * W : 3 * W] = wide(here_count)
    send_all(got1, 1)

    for h in range(hops):
        if h != 1:
            window = slice(win_start(h), win_start(h) + WIN)
            products = dot3(xh[window, :], xl[window, :], xh[window, :], xl[window, :], NT)
        start = h * width - win_start(h)
        hop_grad[0:WIN, :] = products
        part = pltpu.roll(hop_grad[start : start + 104, :], (WIN - start) % WIN, 1)
        ext[GRAM : GRAM + 104, h * 128 : (h + 1) * 128] = part[:, 0:128]

    wait_all(got1, 1)

    delta[...] = jnp.zeros_like(delta)
    every_count = got1[:, 1:2, 2 * W : 3 * W]
    vec[0:1, :] = jnp.sum(every_count, axis=0)
    vec[1:2, :] = jnp.sum(every_count * got1[:, 1:2, W : 2 * W], axis=0)
    for h in range(3):
        vec[2 + h : 3 + h, :] = jnp.sum(got1[:, 0:1, h * W : (h + 1) * W], axis=0)
    vec[5:6, :] = jnp.sum(got1[:, 1:2, 0:W], axis=0)

    total = vec[0:1, :]
    total_lane = vec[0:1, 0:128]
    mean_row = vec[1:2, :] / total
    stats[2:3, :] = total

    @pl.loop(0, n, unroll=8)
    def _(d):
        counts = got1[d, 1:2, 2 * W : 3 * W]
        delta[pl.ds(d, 1), :] = (got1[d, 1:2, W : 2 * W] - mean_row) * jnp.sqrt(counts)

    delta[n : n + 1, :] = got1[me, 1:2, W : 2 * W] - mean_row
    for h in range(hops):
        off = jnp.broadcast_to(delta[n : n + 1, :], (8, W))
        off = pltpu.roll(off, (W - h * width) % W, 1)[0:1, 0:128]
        tall = jnp.broadcast_to(off, (128, 128)).T[0:104, :]
        ext[GRAM : GRAM + 104, h * 128 : (h + 1) * 128] += tall * off * here_count
    span = delta.shape[0]
    span_lane = lax.broadcasted_iota(jnp.int32, (W, span), 1)
    for h in range(hops):
        here = slice(h * W, (h + 1) * W)
        wh, wl = pgh[here, 0:WIN], pgh[here, WIN : 2 * WIN]
        dh, dl = split(delta[:, win_start(h) : win_start(h) + WIN])
        apart = dot3(wh, wl, dh, dl, NT)
        between = jnp.sum(jnp.where(span_lane < n, apart * apart, 0.0), axis=1, keepdims=True)
        offset = jnp.sum(jnp.where(span_lane == n, apart, 0.0), axis=1, keepdims=True)
        spread = to_column(vec[2 + h : 3 + h, :]) + between
        inv = lax.rsqrt(spread / total_lane + 1e-05)
        stats[3 + h : 4 + h, :] = to_row(inv)
        scale = 0.5 * par[0, here, :] * inv
        par[1, here, :] = 0.5 * par[1, here, :] + scale * offset
        par[0, here, :] = scale

    def cat_copy(h, b, slot, part):
        ref = (cath, catl)[part]
        return pltpu.make_async_copy(
            ref.at[slot], cat_hbm.at[part, h, b], cat_sem.at[part, slot]
        )

    def cat_load(h, b, slot, part):
        ref = (cath, catl)[part]
        return pltpu.make_async_copy(
            cat_hbm.at[part, h, b], ref.at[slot], cat_sem.at[part, slot]
        )

    def hop_act(h, b, slot):
        for c in range(8):
            sub = slice(c * 64, (c + 1) * 64)
            here = slice(h * W + c * 64, h * W + (c + 1) * 64)
            pre = tab[pl.ds(pl.multiple_of((h * blocks + b) * W + c * 64, 64), 64), :]
            u = pre * wide(par[0, here, :]) + wide(par[1, here, :])
            t = jnp.tanh(u)
            v = u * (t + wide(par[2, here, :]) * (1.0 - t))
            t = jnp.tanh(v)
            high, low = split((v + v) * (t + wide(par[3, here, :]) * (1.0 - t)))
            cath[slot, sub, :] = high
            catl[slot, sub, :] = low

    @pl.loop(0, blocks)
    def _(b):
        at = pl.ds(pl.multiple_of(b * W, W), W)
        for h in range(hops):

            @pl.when(b > 0)
            def _():
                for part in range(2):
                    cat_copy(h, b - 1, h, part).wait()

        for h in range(hops):
            hop_act(h, b, h)
            here = slice(h * W, (h + 1) * W)
            part_sum = dot3(wmh[here, :], wml[here, :], cath[h], catl[h])
            if h == 0:
                x[at, :] = part_sum
            else:
                x[at, :] += part_sum
        for h in range(hops):
            for part in range(2):
                cat_copy(h, b, h, part).start()

    for h in range(hops):
        for part in range(2):
            cat_copy(h, blocks - 1, h, part).wait()

    acc[0] = jnp.zeros((W, 128), F32)

    @pl.loop(0, blocks)
    def _(b):
        at = pl.ds(pl.multiple_of(b * W, W), W)
        acc[0] += fold(x[at, :] * mask[0:1, at])

    mean_here2 = lane_sum(acc[0]) / here_count
    acc[1] = jnp.zeros((W, 128), F32)

    @pl.loop(0, blocks)
    def _(b):
        at = pl.ds(pl.multiple_of(b * W, W), W)
        off = (x[at, :] - wide(mean_here2)) * mask[0:1, at]
        acc[1] += fold(off * off)

    got2[me, 0:1, :] = to_row(mean_here2)
    got2[me, 1:2, :] = to_row(lane_sum(acc[1]))
    send_all(got2, 2)

    plain_load.wait()
    for h in range(hops):
        high, low = split(dwm[h * W : (h + 1) * W, :])
        wmh[h * W : (h + 1) * W, :] = high
        wml[h * W : (h + 1) * W, :] = low

    classes = bias.shape[1]
    kinds = 48
    ext[SMALL : SMALL + kinds, :] = jnp.zeros((kinds, W), F32)
    ext[SMALL : SMALL + classes, :] = out_t[...]
    oh, ol = split(ext[SMALL : SMALL + kinds, :])
    nh, nl = split(ext[SMALL : SMALL + kinds, :].T)
    vec[6:7, :] = jnp.zeros((1, W), F32)
    vec[6:7, 0:classes] = bias[...]
    bias_col = wide(to_column(vec[6:7, 0:128])[0:kinds, :])

    wait_all(got2, 2)
    every_count = got1[:, 1:2, 2 * W : 3 * W]
    mean2 = jnp.sum(got2[:, 0:1, :] * every_count, axis=0) / total
    off = got2[:, 0:1, :] - mean2
    vec[3:4, :] = jnp.sum(got2[:, 1:2, :] + off * off * every_count, axis=0)
    inv2 = lax.rsqrt(vec[3:4, :] / total + 1e-05)
    mcol[3] = to_column(mean2)
    mcol[4] = to_column(inv2)
    mcol[2] = 0.5 + 0.5 * mcol[2]

    for b in range(blocks):
        for part in range(2):
            cat_load(0, b, b % 4, part).start()

    for j in range(4):
        acc[j] = jnp.zeros((W, 128), F32)
    ext[SMALL : SMALL + 64, :] = jnp.zeros((64, W), F32)
    kind = lax.broadcasted_iota(jnp.int32, (kinds, W), 0)

    @pl.loop(0, blocks)
    def _(b):
        at = pl.ds(pl.multiple_of(b * W, W), W)
        live = mask[0:1, at]
        normed = (x[at, :] - wide(mcol[3])) * wide(mcol[4])
        v = 0.5 * (normed * wide(mcol[0]) + wide(mcol[1]))
        t = jnp.tanh(v)
        keep = wide(mcol[2])
        rest = 1.0 - t
        ah, al = split((v + v) * (t + keep * rest))
        q = v * rest
        logits = dot3(oh, ol, ah, al) + bias_col
        logits = jnp.where(kind < classes, logits, -1e30)
        top = jnp.max(logits, axis=0, keepdims=True)
        e = jnp.exp(logits - top)
        norm = jnp.sum(e, axis=0, keepdims=True)
        logp = logits - top - jnp.log(norm)
        hit = kind == lab[0:1, at]
        loss = jnp.sum(jnp.where(hit, logp, 0.0), axis=0, keepdims=True) * live
        back = (e / norm - jnp.where(hit, 1.0, 0.0)) * (live / total)
        bh, bl = split(back)
        ext[SMALL : SMALL + kinds, :] += dot3(bh, bl, ah, al, NT)
        ext[SMALL + 49 : SMALL + 50, :] -= loss
        acc[3, 0:kinds, :] += fold(back)
        grad = dot3(nh, nl, bh, bl)
        acc[0] += fold(grad * q)
        m = t + q + q * t
        grad = grad * (m + keep * (1.0 - m))
        dwm[at, :] = grad
        acc[1] += fold(grad)
        acc[2] += fold(grad * normed)

    ext[SMALL + 48 : SMALL + 49, :] = to_row(lane_sum(acc[0]))
    ext[SMALL + 50 : SMALL + 51, 0:128] = to_row(lane_sum(acc[3])[0:128, :])
    got3[me, 0:1, :] = to_row(lane_sum(acc[1]))
    got3[me, 1:2, :] = to_row(lane_sum(acc[2]))
    send_all(got3, 3)
    wait_all(got3, 3)
    vec[2:4, :] = jnp.sum(got3[...], axis=0)
    stats[0:2, :] = vec[2:4, :]
    shift_part = to_column(vec[2:3, :] / total)
    gain_part = to_column(vec[3:4, :] / total)
    factor = mcol[0] * mcol[4]

    @pl.loop(0, blocks)
    def _(b):
        at = pl.ds(pl.multiple_of(b * W, W), W)
        normed = (x[at, :] - wide(mcol[3])) * wide(mcol[4])
        grad = dwm[at, :] - wide(shift_part) - normed * wide(gain_part)
        high, low = split(grad * wide(factor) * mask[0:1, at])
        pgh[at, :] = high
        pgl[at, :] = low

    bits = n.bit_length() - 1

    def bit_of(b):
        return lax.rem(me // (1 << b), 2)

    def across(b):
        return me + (1 << b) * (1 - 2 * bit_of(b))

    def remote(src, dst, send, recv, to):
        return pltpu.make_async_remote_copy(
            src, dst, send, recv, device_id=(to,), device_id_type=MESH
        )

    def wait_bytes(ref, sem):
        pltpu.make_async_copy(ref, ref, sem).wait()

    for b in range(bits):
        pl.semaphore_signal(credit, inc=1, device_id=(across(b),), device_id_type=MESH)

    far = list(range(3, bits))
    orders = [[1] + far + [2], [2] + far + [1]]
    span = W // len(orders)

    def halving(batch, base, size, take):
        def rows_at(off, length):
            return pl.ds(pl.multiple_of(off, 8), length)

        half = size // 2
        tmps = [take(half)]
        levels = [
            [(0, slice(0, W), base + bit_of(0) * half, base + (1 - bit_of(0)) * half, half, tmps[0][1])]
        ]
        rest_tmp, at = take(half)
        tmps += [(rest_tmp, at)] * (bits - 1)
        offs = [base + bit_of(0) * half] * len(orders)
        length = half
        for j in range(bits - 1):
            length //= 2
            level = []
            for q in range(len(orders)):
                b = orders[q][j]
                keep = offs[q] + bit_of(b) * length
                give = offs[q] + (1 - bit_of(b)) * length
                level.append((b, slice(q * span, (q + 1) * span), keep, give, length, at))
                offs[q] = keep
            at += length
            levels.append(level)

        stages = []
        for k, level in enumerate(levels):
            send, recv = sum_send.at[batch, k], sum_recv.at[batch, k]
            free = freed.at[batch, k]
            length, first = level[0][4:]
            tmp = tmps[k][0]
            arrived = tmp.at[first : first + length, :]

            def start(level=level, send=send, recv=recv, tmp=tmp):
                for b, lanes, keep, give, ln, t in level:
                    remote(
                        dwm.at[rows_at(give, ln), lanes], tmp.at[t : t + ln, lanes],
                        send, recv, across(b),
                    ).start()

            def finish(level=level, send=send, recv=recv, free=free, arrived=arrived, tmp=tmp):
                wait_bytes(arrived, send)
                wait_bytes(arrived, recv)
                for b, lanes, keep, give, ln, t in level:
                    pl.semaphore_signal(
                        free, inc=1, device_id=(across(b),), device_id_type=MESH
                    )
                    dwm[rows_at(keep, ln), lanes] += tmp[t : t + ln, lanes]

            stages.append((start, finish))
        for k in range(bits - 1, -1, -1):
            level = levels[k]
            send, recv = sum_send.at[batch, bits + k], sum_recv.at[batch, bits + k]
            free = freed.at[batch, k]
            length, first = level[0][4:]
            arrived = tmps[k][0].at[first : first + length, :]

            def start(level=level, send=send, recv=recv, free=free):
                pl.semaphore_wait(free, len(level))
                for b, lanes, keep, give, ln, t in level:
                    here = dwm.at[rows_at(keep, ln), lanes]
                    remote(here, here, send, recv, across(b)).start()

            def finish(send=send, recv=recv, arrived=arrived):
                wait_bytes(arrived, send)
                wait_bytes(arrived, recv)

            stages.append((start, finish))
        return stages

    chips = n // 2
    core, chip = lax.rem(me, 2), me // 2
    half_lanes = W // 2
    mine = pl.ds(pl.multiple_of(core * half_lanes, 128), half_lanes)
    other = pl.ds(pl.multiple_of((1 - core) * half_lanes, 128), half_lanes)

    def direct(batch, base, size, rows_each, tmp_base, tmp_lane):
        owners = size // rows_each
        cols = slice(tmp_lane, tmp_lane + half_lanes)
        block = pl.ds(base, size)
        from_core = tab.at[tmp_base : tmp_base + size, cols]
        first = tmp_base + size
        slot = tab.at[pl.ds(pl.multiple_of(first + chip * rows_each, 8), rows_each), cols]
        summed = own.at[batch, 0:rows_each, :]
        sends = [part_send.at[batch, k] for k in range(4)]
        recvs = [part_recv.at[batch, k] for k in range(4)]

        def many(k):
            return tab.at[first : first + rows_each * k, cols]

        def piece(q):
            return pl.ds(pl.multiple_of(base + q * rows_each, 8), rows_each)

        def start():
            remote(ext.at[block, other], from_core, sends[0], recvs[0], across(0)).start()

        def spread():
            wait_bytes(from_core, sends[0])
            wait_bytes(from_core, recvs[0])
            ext[block, mine] += tab[tmp_base : tmp_base + size, cols]

            @pl.loop(0, owners)
            def _(k):
                q = lax.rem(chip + k, owners)

                @pl.when(q == chip)
                def _():
                    pltpu.make_async_copy(ext.at[piece(q), mine], slot, recvs[1]).start()

                @pl.when(q != chip)
                def _():
                    remote(ext.at[piece(q), mine], slot, sends[1], recvs[1], q * 2 + core).start()

        def middle():
            @pl.when(chip < owners)
            def _():
                wait_bytes(many(owners - 1), sends[1])
                wait_bytes(many(chips), recvs[1])
                out = tab[first : first + rows_each, cols]
                for d in range(1, chips):
                    at = first + rows_each * d
                    out = out + tab[at : at + rows_each, cols]
                own[batch, 0:rows_each, :] = out
                there = res.at[piece(chip), mine]
                pltpu.make_async_copy(summed, there, recvs[2]).start()

                @pl.loop(1, chips)
                def _(k):
                    to = lax.rem(chip + k, chips) * 2 + core
                    remote(summed, there, sends[2], recvs[2], to).start()

            @pl.when(chip >= owners)
            def _():
                wait_bytes(many(owners), sends[1])

        def join():
            wait_bytes(res.at[block, mine], recvs[2])

            @pl.when(chip < owners)
            def _():
                wait_bytes(many(chips - 1), sends[2])

            here = res.at[block, mine]
            remote(here, here, sends[3], recvs[3], across(0)).start()

        def finish():
            wait_bytes(res.at[block, other], sends[3])
            wait_bytes(res.at[block, other], recvs[3])

        return [start, spread, middle, join, finish]

    mid_batch = max(W, 8 * n)
    mids = hops * W // mid_batch
    DW, HB, GAP = 1.0, 2.1, 4.0
    PART = (2.5, 5.0, 5.0, 2.5)
    clock = [(t + 1) * DW for t in range(hops * blocks)]
    clock += [clock[-1] + (t + 1) * HB for t in range(hops * blocks)]
    spare = hops * rows
    part_rows = 208 + 16 * chips
    spots = [(x, W, x.shape[0] - W), (tab, spare + part_rows, tab.shape[0] - spare - part_rows)]

    def take(size):
        spot = next(i for i in range(2) if spots[i][2] >= size)
        ref, first, left = spots[spot]
        spots[spot] = (ref, first + size, left - size)
        return ref, first

    events = []
    for k in range(mids):
        stages = halving(k, k * mid_batch, mid_batch, take)
        when = clock[(k + 1) * mid_batch // W * blocks - 1]
        for j in range(len(stages) + 1):
            todo = []
            if j:
                todo.append(stages[j - 1][1])
            elif k == 0:
                todo.append(lambda: pl.semaphore_wait(credit, bits))
            if j < len(stages):
                todo.append(stages[j][0])
            else:
                todo.append(lambda k=k: mid_out(k).start())
            events.append((when, len(events), todo))
            when += GAP
    ends = [clock[hops * blocks + (h + 1) * blocks - 1] for h in range(hops)]
    for batch, (when, base, size, rows_each) in enumerate(
        (
            (clock[0], 0, HOPS_AT, 16),
            (ends[1], hop_row(0), 208, 16),
            (ends[2], hop_row(2), 104, 8),
            (ends[3], hop_row(3), 104, 8),
        )
    ):
        stages = direct(batch, base, size, rows_each, spare, batch % 2 * half_lanes)
        for j, stage in enumerate(stages):
            at = when + sum(PART[:j])
            if batch == 1:
                at = min(at, ends[3] - 1e-3)
            events.append((at, len(events), [stage]))

    ticks = {}
    for when, _, todo in sorted(events, key=lambda e: e[:2]):
        tick = next((t for t, c in enumerate(clock) if c >= when - 1e-6), len(clock))
        ticks.setdefault(tick, []).extend(todo)

    def mid_out(k):
        here = slice(k * mid_batch, (k + 1) * mid_batch)
        return pltpu.make_async_copy(dwm.at[here], mid_sum.at[here], table_sem.at[k])

    def act(tick):
        for todo in ticks.get(tick, []):
            todo()

    for h in range(hops):
        here = slice(h * W, (h + 1) * W)

        @pl.loop(0, blocks)
        def _(b):
            at = pl.ds(pl.multiple_of(b * W, W), W)
            slot = lax.rem(b, 4)
            for part in range(2):
                cat_load(h, b, slot, part).wait()
            part_sum = dot3(cath[slot], catl[slot], pgh[at, :], pgl[at, :], NT)
            if h + 1 < hops:
                for part in range(2):
                    cat_load(h + 1, b, slot, part).start()

            @pl.when(b == 0)
            def _():
                dwm[here, :] = part_sum

            @pl.when(b > 0)
            def _():
                dwm[here, :] += part_sum

            for t in range(blocks):
                if ticks.get(h * blocks + t):

                    @pl.when(b == t)
                    def _():
                        act(h * blocks + t)

    grads = (x.at[0:W], cg)

    def head_back(h, b, rs):
        at = pl.ds(b * W, W)
        here = pl.ds(pl.multiple_of(h * W + rs.start, 128), rs.stop - rs.start)
        return dot3(wmh[here, :], wml[here, :], pgh[at, :], pgl[at, :])

    def weight_back(h, b, rs):
        window = pl.ds(pl.multiple_of(jnp.maximum(h - 1, 0) * 128, 128), WIN)
        at = pl.ds(b * W, W)
        part_sum = dot3(
            cath[b % 2, rs, :], catl[b % 2, rs, :], xh[window, at], xl[window, at], NT
        )
        if b == 0:
            hop_grad[rs, :] = part_sum
        else:
            hop_grad[rs, :] += part_sum

    def act_back(h, b, c):
        sub = slice(c * 64, (c + 1) * 64)
        col = pl.ds(pl.multiple_of(h * W + c * 64, 64), 64)
        grad = grads[b % 2][sub, :]
        pre = tab[pl.ds(pl.multiple_of((h * blocks + b) * W + c * 64, 64), 64), :]
        keep1, keep2 = wide(par[2, col, :]), wide(par[3, col, :])
        u = pre * wide(par[0, col, :]) + wide(par[1, col, :])
        t1 = jnp.tanh(u)
        r1 = 1.0 - t1
        v = u * (t1 + keep1 * r1)
        t2 = jnp.tanh(v)
        q = v * (1.0 - t2)
        sum2 = fold(grad * q)
        m = t2 + q + q * t2
        grad = grad * (m + keep2 * (1.0 - m))
        q = u * r1
        sum1 = fold(grad * q)
        m = t1 + q + q * t1
        grad = grad * (m + keep1 * (1.0 - m))
        for j, value in enumerate((sum2, sum1, fold(grad))):
            if b == 0:
                acc[j, sub, :] = value
            else:
                acc[j, sub, :] += value
        high, low = split(grad)
        cath[b % 2, sub, :] = high
        catl[b % 2, sub, :] = low

    halves = (slice(0, W // 2), slice(W // 2, W))
    grads[0][...] = head_back(0, 0, slice(0, W))

    @pl.loop(0, hops)
    def _(h):
        for b in range(blocks):
            for m, rs in enumerate(halves):
                if b + 1 < blocks:
                    grads[(b + 1) % 2][rs, :] = head_back(h, b + 1, rs)
                else:
                    grads[(b + 1) % 2][rs, :] = head_back(jnp.minimum(h + 1, hops - 1), 0, rs)
                if b:
                    weight_back(h, b - 1, rs)
                for c in range(4 * m, 4 * m + 4):
                    act_back(h, b, c)
            if b + 1 < blocks:
                for t in range(hops):
                    if ticks.get(hops * blocks + t * blocks + b):

                        @pl.when(h == t)
                        def _():
                            act(hops * blocks + t * blocks + b)

        weight_back(h, blocks - 1, slice(0, W))
        for t in range(hops):

            @pl.when(h == t)
            def _():
                sums = lane_sum(acc[2])
                offset = delta[n : n + 1, win_start(t) : win_start(t) + WIN]
                tall = hop_grad[...] + jnp.concatenate([sums] * 2, axis=1) * offset
                first = hop_row(t)
                start = t * width - win_start(t)
                cg[0:WIN, :] = tall.T
                ext[first : first + width, :] = cg[start : start + width, :]
                for j in range(3):
                    row = first + width + j
                    ext[row : row + 1, :] = to_row(lane_sum(acc[j]))
                act(hops * blocks + t * blocks + blocks - 1)

    act(len(clock))
    rest_out = pltpu.make_async_copy(res, rest_sum, load_sem.at[0])
    rest_out.start()
    for k in range(mids):
        mid_out(k).wait()
    rest_out.wait()


GRAM, SMALL, HOPS_AT = 0, 104, 176


def hop_row(h):
    return HOPS_AT + h * 104


def final_kernel(
    mid_sum, rest, stats, weights, gain, loss, hop_w, hop_g, hop_s, hop_l, cat_l, mid_w,
    mid_g, mid_s, mid_l, out_w, out_b, buf, wide_w, sem,
):
    parts = 4
    size = mid_sum.shape[0] // parts

    def load(k):
        here = slice(k * size, (k + 1) * size)
        return pltpu.make_async_copy(mid_sum.at[here], buf.at[here], sem.at[0, k])

    def store(k):
        here = slice(k * size, (k + 1) * size)
        return pltpu.make_async_copy(buf.at[here], mid_w.at[here], sem.at[1, k])

    for k in range(parts):
        load(k).start()
    total = stats[2:3, :]
    width, hops, _ = weights.shape
    wide_w[...] = jnp.zeros_like(wide_w)
    for h in range(hops):
        first = hop_row(h)
        raw = rest[first : first + width, :]
        weight = weights[:, h, :]
        inv = stats[3 + h : 4 + h, :]
        gain_grad = inv * jnp.sum(weight * raw, axis=0, keepdims=True)
        wide_w[0:width, :] = weight
        along = lax.dot_general(
            rest[GRAM : GRAM + 104, h * 128 : (h + 1) * 128], wide_w[...], NN,
            precision=lax.Precision.HIGHEST, preferred_element_type=F32,
        )[0:width, :]
        grad = raw - along * (inv * gain_grad / total)
        hop_w[:, h, :] = gain[h : h + 1, :] * inv * grad
        hop_g[h : h + 1, :] = gain_grad
        cat_l[0:1, h * W : (h + 1) * W] = rest[first + width : first + width + 1, :]
        hop_l[h : h + 1, :] = rest[first + width + 1 : first + width + 2, :]
        hop_s[h : h + 1, :] = rest[first + width + 2 : first + width + 3, :]
        load(h).wait()
        store(h).start()
    mid_s[...] = stats[0:1, :]
    mid_g[...] = stats[1:2, :]
    mid_l[...] = rest[SMALL + 48 : SMALL + 49, :]
    out_w[...] = rest[SMALL : SMALL + out_w.shape[0], :]
    out_b[...] = rest[SMALL + 50 : SMALL + 51, 0 : out_b.shape[1]]
    loss[...] = jnp.sum(rest[SMALL + 49 : SMALL + 50, :], axis=1, keepdims=True) / total[:, 0:1]
    for k in range(parts):
        store(k).wait()


def on_device(
    node_table, batch_nodes, send_counts, labels, hop_weight, hop_gain, hop_shift, hop_slope,
    cat_slope, mid_weight, mid_gain, mid_shift, mid_slope, out_weight, out_bias,
):
    n = lax.axis_size("nodes")
    node_rows, feats = node_table.shape
    rows = batch_nodes.shape[0]
    slots = rows // n
    hops, width, units = hop_weight.shape
    blocks = rows // W
    classes = out_weight.shape[1]
    vmem = pl.BlockSpec(memory_space=pltpu.VMEM)
    hbm = pl.BlockSpec(memory_space=pl.ANY)
    shape = jax.ShapeDtypeStruct
    bits = n.bit_length() - 1
    mid_batch = max(W, 8 * n)
    sums = hops * W // mid_batch
    small_rows = HOPS_AT + 104 * hops
    halves = 2 * sums - (hops * W - W) // (mid_batch // 2)
    spill = 208 + 8 * n + halves * mid_batch // 2
    tab_rows = max(node_rows, hops * rows + spill)
    weights = hop_weight.transpose(1, 0, 2)
    mid_sum, rest_sum, stats, _ = pl.pallas_call(
        functools.partial(main_kernel, n, slots),
        out_shape=(
            shape((hops * units, W), F32),
            shape((small_rows, W), F32),
            shape((8, W), F32),
            shape((2, hops, blocks, W, W), BF16),
        ),
        in_specs=[hbm, vmem, vmem, pl.BlockSpec(memory_space=pltpu.SMEM), vmem, hbm] + [vmem] * 9,
        out_specs=(hbm, hbm, vmem, hbm),
        scratch_shapes=[
            pltpu.VMEM((tab_rows, 512), F32),
            pltpu.VMEM((max(rows, hops * W), W), F32),
            pltpu.VMEM((max(rows, hops * W), W), F32),
            pltpu.VMEM((512, rows), BF16),
            pltpu.VMEM((512, rows), BF16),
            pltpu.VMEM((hops * W, W), BF16),
            pltpu.VMEM((hops * W, W), BF16),
            pltpu.VMEM((max(rows, hops * W), W), BF16),
            pltpu.VMEM((max(rows, hops * W), W), BF16),
            pltpu.VMEM((4, W, W), BF16),
            pltpu.VMEM((4, W, W), BF16),
            pltpu.VMEM((4, hops * W, 128), F32),
            pltpu.VMEM((5, W, 128), F32),
            pltpu.VMEM((4, W, 128), F32),
            pltpu.VMEM((8, W), F32),
            pltpu.VMEM((1, rows), F32),
            pltpu.VMEM((1, rows), jnp.int32),
            pltpu.VMEM((n + 8, W), F32),
            pltpu.VMEM((small_rows, W), F32),
            pltpu.VMEM((small_rows, W), F32),
            pltpu.VMEM((4, 16, W // 2), F32),
            pltpu.VMEM((W, WIN), F32),
            pltpu.VMEM((W, W), F32),
            pltpu.SMEM((n, 2, 128), jnp.int32),
            pltpu.VMEM((n, 2, 128), jnp.int32),
            pltpu.VMEM((n, 2, 128), jnp.int32),
            pltpu.VMEM((n, 2, 3 * W), F32),
            pltpu.VMEM((n, 2, W), F32),
            pltpu.VMEM((n, 2, W), F32),
            pltpu.SemaphoreType.DMA((4,)),
            pltpu.SemaphoreType.DMA((4,)),
            pltpu.SemaphoreType.DMA((sums, 2 * bits)),
            pltpu.SemaphoreType.DMA((sums, 2 * bits)),
            pltpu.SemaphoreType.DMA((4, 4)),
            pltpu.SemaphoreType.DMA((4, 4)),
            pltpu.SemaphoreType.REGULAR,
            pltpu.SemaphoreType.REGULAR((sums, bits)),
            pltpu.SemaphoreType.DMA((8,)),
            pltpu.SemaphoreType.DMA((2,)),
            pltpu.SemaphoreType.DMA((2, 4)),
        ],
        compiler_params=pltpu.CompilerParams(
            collective_id=0, has_side_effects=True, vmem_limit_bytes=66_900_000
        ),
    )(
        node_table.T, batch_nodes.reshape(rows // 128, 128), labels.reshape(rows // 128, 128),
        send_counts, weights, mid_weight, hop_gain, hop_shift, hop_slope,
        cat_slope.reshape(1, hops * units), mid_gain.reshape(1, W), mid_shift.reshape(1, W),
        mid_slope.reshape(1, W), out_weight.T, out_bias.reshape(1, classes),
    )
    (
        loss, hop_w, hop_g, hop_s, hop_l, cat_l, mid_w, mid_g, mid_s, mid_l, out_w, out_b,
    ) = pl.pallas_call(
        final_kernel,
        out_shape=(
            shape((1, 1), F32), shape((width, hops, units), F32), shape((hops, units), F32),
            shape((hops, units), F32), shape((hops, units), F32), shape((1, hops * units), F32),
            shape((hops * units, W), F32), shape((1, W), F32), shape((1, W), F32),
            shape((1, W), F32), shape((classes, W), F32), shape((1, classes), F32),
        ),
        in_specs=[hbm] + [vmem] * 4,
        out_specs=(vmem,) * 6 + (hbm,) + (vmem,) * 5,
        scratch_shapes=[
            pltpu.VMEM((hops * units, W), F32),
            pltpu.VMEM((128, W), F32),
            pltpu.SemaphoreType.DMA((2, 4)),
        ],
        compiler_params=pltpu.CompilerParams(vmem_limit_bytes=32 * 2**20),
    )(mid_sum, rest_sum, stats, weights, hop_gain)
    return (
        loss.reshape(()), hop_w.transpose(1, 0, 2), hop_g, hop_s, hop_l, cat_l.reshape(-1),
        mid_w, mid_g.reshape(-1), mid_s.reshape(-1), mid_l.reshape(-1), out_w.T,
        out_b.reshape(-1),
    )


def solution(mesh):
    placed = (P("nodes", None), P("nodes"), P("nodes", None), P("nodes")) + (P(),) * 11
    return jax.shard_map(
        on_device, mesh=mesh, in_specs=placed, out_specs=(P(),) * 12, check_vma=False
    )
```

profile of v0, /device:TPU:0, one launch (start us, length us, event | category | flops | bytes accessed | tf_op | source)
XLA Modules:
  0.0 203.0 jit_solution(16920878145639574477)
XLA Ops:
  0.6 0.0 copy-start.3
  0.7 192.9 %shard_map.238 = (f32[2048,512]{1,0:T(8,128)}, f32[592,512]{1,0:T(8,128)}, f32[8,512]{1,0:T(8,128)}, bf16[2,4,4,512,512]{4,3,2,1,0:T(8,128)(2,1)}) custom-call(f32[400,9600]{1,0:T(8,128)} %bitcast.20, s32[16,128]{1,0:T(8,128)} %bitcast.22, s32[16,128]{1,0:T(8,128)} %bitcast.23, s32[1,32]{1,0:T(1,128)} %counts.1, f32[100,4,512]{2,1,0:T(4,128)} %bitcast.18, ...), custom_call_target="tpu_custom_call" | custom-call | tf_op jit(solution)/shard_map/pallas_call | solution.py:967
  193.5 0.0 copy-done.3
  193.6 0.0 copy-start
  193.6 2.2 %copy-done = f32[2048,512]{1,0:T(8,128)S(1)} copy-done((f32[2048,512]{1,0:T(8,128)S(1)}, f32[2048,512]{1,0:T(8,128)}, u32[]{:S(2)}) %copy-start) | copy-done | bytes 4194328
  195.7 0.0 copy-start.1
  195.8 1.1 copy-done.1
  196.9 0.0 copy-start.2
  196.9 1.3 copy-done.2
  198.2 0.0 copy-start.4
  198.2 0.7 copy-done.4
  198.9 4.0 %shard_map.239 = (f32[1,1]{1,0:T(1,128)}, f32[100,4,512]{2,1,0:T(4,128)}, f32[4,512]{1,0:T(4,128)}, f32[4,512]{1,0:T(4,128)}, f32[4,512]{1,0:T(4,128)}, /*index=...) custom-call(f32[2048,512]{1,0:T(8,128)S(1)} %copy-done, ...), custom_call_target="tpu_custom_call" | custom-call | tf_op jit(solution)/shard_map/pallas_call | solution.py:1030
Async XLA Ops:
  0.6 192.9 %copy-start.3 = (f32[4,512]{1,0:T(4,128)S(1)}, f32[4,512]{1,0:T(4,128)}, u32[]{:S(2)}) copy-start(f32[4,512]{1,0:T(4,128)} %gain.3) | copy-start | bytes 24580
  193.6 2.2 %copy-start = (f32[2048,512]{1,0:T(8,128)S(1)}, f32[2048,512]{1,0:T(8,128)}, u32[]{:S(2)}) copy-start(f32[2048,512]{1,0:T(8,128)} %get-tuple-element.27.mid_sum) | copy-start | bytes 12582916
  195.7 1.1 copy-start.1
  196.9 1.3 copy-start.2
  198.2 0.7 copy-start.4
where the time goes:
time: 203 us
  Pallas kernels  197 us (97%)
  local copies, waits for them, and re-layouts  5.33 us (3%)
    pallas_call x1, Pallas kernels, on_device(): pl.pallas_call(functools.partial(main_kernel, n, slots), out_shape=(shape...  193 us
    unnamed x10, local copies, waits for them, and re-layouts  5.33 us

commit v1 on v0

--- a/solution.py
+++ b/solution.py
@@ -237,15 +237,17 @@
     to_smem.start()
     to_smem.wait()
 
-    step = min(slots, 16)
+    step = min(slots, 32)
 
     @pl.loop(0, n)
     def _(s):
         @pl.loop(0, slots // step)
         def _(g):
-            for k in range(step):
-                at = g * step + k
-                x[pl.ds(s * slots + at, 1), :] = tab[pl.ds(ids[s, 0, at], 1), :]
+            for first in range(0, step, 8):
+                at = g * step + first
+                x[pl.ds(pl.multiple_of(s * slots + at, 8), 8), :] = jnp.concatenate(
+                    [tab[pl.ds(ids[s, 0, at + k], 1), :] for k in range(8)], axis=0
+                )
 
     @pl.loop(0, rows // 128)
     def _(j):
@@ -301,7 +303,7 @@
         window = slice(win_start(h), win_start(h) + WIN)
         acc[h] = jnp.zeros((W, 128), F32)
 
-        @pl.loop(0, blocks)
+        @pl.loop(0, blocks, unroll=4)
         def _(b):
             at = pl.ds(pl.multiple_of(b * W, W), W)
             pre = dot3(wh, wl, xh[window, at], xl[window, at])
@@ -406,15 +408,14 @@
 
         for h in range(hops):
             hop_act(h, b, h)
+            for part in range(2):
+                cat_copy(h, b, h, part).start()
             here = slice(h * W, (h + 1) * W)
             part_sum = dot3(wmh[here, :], wml[here, :], cath[h], catl[h])
             if h == 0:
                 x[at, :] = part_sum
             else:
                 x[at, :] += part_sum
-        for h in range(hops):
-            for part in range(2):
-                cat_copy(h, b, h, part).start()
 
     for h in range(hops):
         for part in range(2):
@@ -548,7 +549,7 @@
         pl.semaphore_signal(credit, inc=1, device_id=(across(b),), device_id_type=MESH)
 
     far = list(range(3, bits))
-    orders = [[1] + far + [2], [2] + far + [1]]
+    orders = [[1, 2] + far, [2, 1] + far, [1] + far + [2], [2] + far + [1]]
     span = W // len(orders)
 
     def halving(batch, base, size, take):
@@ -704,7 +705,7 @@
 
     mid_batch = max(W, 8 * n)
     mids = hops * W // mid_batch
-    DW, HB, GAP = 1.0, 2.1, 4.0
+    DW, HB, GAP = 1.0, 2.1, 4.5
     PART = (2.5, 5.0, 5.0, 2.5)
     clock = [(t + 1) * DW for t in range(hops * blocks)]
     clock += [clock[-1] + (t + 1) * HB for t in range(hops * blocks)]
@@ -894,8 +895,8 @@
 
 
 def final_kernel(
-    mid_sum, rest, stats, weights, gain, loss, hop_w, hop_g, hop_s, hop_l, cat_l, mid_w,
-    mid_g, mid_s, mid_l, out_w, out_b, buf, wide_w, sem,
+    mid_sum, rest_sum, stats_sum, weights_in, gain, loss, hop_w, hop_g, hop_s, hop_l, cat_l, mid_w,
+    mid_g, mid_s, mid_l, out_w, out_b, buf, wide_w, rest, stats, weights, sem,
 ):
     parts = 4
     size = mid_sum.shape[0] // parts
@@ -908,8 +909,16 @@
         here = slice(k * size, (k + 1) * size)
         return pltpu.make_async_copy(buf.at[here], mid_w.at[here], sem.at[1, k])
 
+    loads = [
+        pltpu.make_async_copy(src, dst, sem.at[2, k])
+        for k, (src, dst) in enumerate(((rest_sum, rest), (stats_sum, stats), (weights_in, weights)))
+    ]
+    for copy in loads:
+        copy.start()
     for k in range(parts):
         load(k).start()
+    for copy in loads:
+        copy.wait()
     total = stats[2:3, :]
     width, hops, _ = weights.shape
     wide_w[...] = jnp.zeros_like(wide_w)
@@ -1035,14 +1044,17 @@
             shape((hops * units, W), F32), shape((1, W), F32), shape((1, W), F32),
             shape((1, W), F32), shape((classes, W), F32), shape((1, classes), F32),
         ),
-        in_specs=[hbm] + [vmem] * 4,
+        in_specs=[hbm] * 4 + [vmem],
         out_specs=(vmem,) * 6 + (hbm,) + (vmem,) * 5,
         scratch_shapes=[
             pltpu.VMEM((hops * units, W), F32),
             pltpu.VMEM((128, W), F32),
-            pltpu.SemaphoreType.DMA((2, 4)),
+            pltpu.VMEM((small_rows, W), F32),
+            pltpu.VMEM((8, W), F32),
+            pltpu.VMEM((width, hops, units), F32),
+            pltpu.SemaphoreType.DMA((3, 4)),
         ],
-        compiler_params=pltpu.CompilerParams(vmem_limit_bytes=32 * 2**20),
+        compiler_params=pltpu.CompilerParams(vmem_limit_bytes=62 * 2**20),
     )(mid_sum, rest_sum, stats, weights, hop_gain)
     return (
         loss.reshape(()), hop_w.transpose(1, 0, 2), hop_g, hop_s, hop_l, cat_l.reshape(-1),

time: 203 us -> 201 us (level); the launches traced: 203 us -> 198 us
  local copies, waits for them, and re-layouts: 5.33 us -> 0 us
    unnamed x10 -> x0, local copies, waits for them, and re-layouts: 5.33 us -> none
where the time goes in v1:
time: 201 us; the launch traced here: 198 us
  Pallas kernels  197 us (98%)
    pallas_call x1, Pallas kernels, on_device(): pl.pallas_call(functools.partial(main_kernel, n, slots), out_shape=(shape...  191 us
    pallas_call x1, Pallas kernels, on_device(): pl.pallas_call(final_kernel, out_shape=(shape((1, 1), F32), shape((width,...  5.91 us

profile of v1, /device:TPU:0, one launch (start us, length us, event | category | flops | bytes accessed | tf_op | source)
XLA Modules:
  0.0 197.9 jit_solution(9397160536617001781)
XLA Ops:
  0.6 191.1 %shard_map.238 = (f32[2048,512]{1,0:T(8,128)}, f32[592,512]{1,0:T(8,128)}, f32[8,512]{1,0:T(8,128)}, bf16[2,4,4,512,512]{4,3,2,1,0:T(8,128)(2,1)}) custom-call(f32[400,9600]{1,0:T(8,128)} %bitcast.18, s32[16,128]{1,0:T(8,128)} %bitcast.22, s32[16,128]{1,0:T(8,128)} %bitcast.23, s32[1,32]{1,0:T(1,128)} %counts.1, f32[100,4,512]{2,1,0:T(4,128)} %bitcast.19, ...), custom_call_target="tpu_custom_call" | custom-call | tf_op jit(solution)/shard_map/pallas_call | solution.py:976
  191.8 5.9 %shard_map.239 = (f32[1,1]{1,0:T(1,128)}, f32[100,4,512]{2,1,0:T(4,128)}, f32[4,512]{1,0:T(4,128)}, f32[4,512]{1,0:T(4,128)}, f32[4,512]{1,0:T(4,128)}, /*index=...) custom-call(f32[2048,512]{1,0:T(8,128)} %get-tuple-element.27.mid_su, ...), custom_call_target="tpu_custom_call" | custom-call | tf_op jit(solution)/shard_map/pallas_call | solution.py:1039

commit v2 on v1

--- a/solution.py
+++ b/solution.py
@@ -706,7 +706,7 @@
     mid_batch = max(W, 8 * n)
     mids = hops * W // mid_batch
     DW, HB, GAP = 1.0, 2.1, 4.5
-    PART = (2.5, 5.0, 5.0, 2.5)
+    PART = (4.2, 6.3, 6.3, 4.2)
     clock = [(t + 1) * DW for t in range(hops * blocks)]
     clock += [clock[-1] + (t + 1) * HB for t in range(hops * blocks)]
     spare = hops * rows

time: 201 us -> 199 us (0.990)
    pallas_call x1, Pallas kernels: 191 us -> 189 us  [on_device(): pl.pallas_call(functools.partial(main_kernel, n, slots), out_shape=(shape...]
where the time goes in v2:
time: 199 us; the launch traced here: 196 us
  Pallas kernels  195 us (98%)
    pallas_call x1, Pallas kernels, on_device(): pl.pallas_call(functools.partial(main_kernel, n, slots), out_shape=(shape...  189 us
    pallas_call x1, Pallas kernels, on_device(): pl.pallas_call(final_kernel, out_shape=(shape((1, 1), F32), shape((width,...  5.91 us

profile of v2, /device:TPU:0, one launch (start us, length us, event | category | flops | bytes accessed | tf_op | source)
XLA Modules:
  0.0 195.6 jit_solution(8693092434414808819)
XLA Ops:
  0.6 188.8 %shard_map.238 = (f32[2048,512]{1,0:T(8,128)}, f32[592,512]{1,0:T(8,128)}, f32[8,512]{1,0:T(8,128)}, bf16[2,4,4,512,512]{4,3,2,1,0:T(8,128)(2,1)}) custom-call(f32[400,9600]{1,0:T(8,128)} %bitcast.18, s32[16,128]{1,0:T(8,128)} %bitcast.22, s32[16,128]{1,0:T(8,128)} %bitcast.23, s32[1,32]{1,0:T(1,128)} %counts.1, f32[100,4,512]{2,1,0:T(4,128)} %bitcast.19, ...), custom_call_target="tpu_custom_call" | custom-call | tf_op jit(solution)/shard_map/pallas_call | solution.py:976
  189.5 5.9 %shard_map.239 = (f32[1,1]{1,0:T(1,128)}, f32[100,4,512]{2,1,0:T(4,128)}, f32[4,512]{1,0:T(4,128)}, f32[4,512]{1,0:T(4,128)}, f32[4,512]{1,0:T(4,128)}, /*index=...) custom-call(f32[2048,512]{1,0:T(8,128)} %get-tuple-element.27.mid_su, ...), custom_call_target="tpu_custom_call" | custom-call | tf_op jit(solution)/shard_map/pallas_call | solution.py:1039

commit v3 on v2

--- a/solution.py
+++ b/solution.py
@@ -141,7 +141,7 @@
         )
 
     def send_all(buf, e):
-        @pl.loop(1, n)
+        @pl.loop(1, n, unroll=n - 1)
         def _(k):
             pltpu.make_async_remote_copy(
                 buf.at[me], buf.at[me], send_sem.at[e], recv_sem.at[e],

time: 199 us -> 199 us (level)
  no operation moved by 1% of the time
where the time goes in v3:
time: 199 us; the launch traced here: 195 us
  Pallas kernels  195 us (98%)
    pallas_call x1, Pallas kernels, on_device(): pl.pallas_call(functools.partial(main_kernel, n, slots), out_shape=(shape...  189 us
    pallas_call x1, Pallas kernels, on_device(): pl.pallas_call(final_kernel, out_shape=(shape((1, 1), F32), shape((width,...  5.91 us

profile of v3, /device:TPU:0, one launch (start us, length us, event | category | flops | bytes accessed | tf_op | source)
XLA Modules:
  0.0 195.5 jit_solution(4946694443888562769)
XLA Ops:
  0.6 188.7 %shard_map.238 = (f32[2048,512]{1,0:T(8,128)}, f32[592,512]{1,0:T(8,128)}, f32[8,512]{1,0:T(8,128)}, bf16[2,4,4,512,512]{4,3,2,1,0:T(8,128)(2,1)}) custom-call(f32[400,9600]{1,0:T(8,128)} %bitcast.18, s32[16,128]{1,0:T(8,128)} %bitcast.22, s32[16,128]{1,0:T(8,128)} %bitcast.23, s32[1,32]{1,0:T(1,128)} %counts.1, f32[100,4,512]{2,1,0:T(4,128)} %bitcast.19, ...), custom_call_target="tpu_custom_call" | custom-call | tf_op jit(solution)/shard_map/pallas_call | solution.py:976
  189.4 5.9 %shard_map.239 = (f32[1,1]{1,0:T(1,128)}, f32[100,4,512]{2,1,0:T(4,128)}, f32[4,512]{1,0:T(4,128)}, f32[4,512]{1,0:T(4,128)}, f32[4,512]{1,0:T(4,128)}, /*index=...) custom-call(f32[2048,512]{1,0:T(8,128)} %get-tuple-element.27.mid_su, ...), custom_call_target="tpu_custom_call" | custom-call | tf_op jit(solution)/shard_map/pallas_call | solution.py:1039
